TPU v7x, 32 devices: a whole 2x2x4 slice. The times are simulated.
32 devices in a mesh: group: 2 (over x), src: 8 (over z, y), tile: 2 (over core).
Axes of the slice: x: 2, y: 2, z: 4, core: 2. Of those that a mesh axis runs over, the one named last changes fastest.
Arguments:
- near_field: bfloat16 [4, 64, 2, 3, 512], P(('group', 'tile'), 'src'), parts along dimension 0, may hold values from -6 to 6
- x_taps: bfloat16 [8, 2, 8, 65], P('src'), may hold values from -0.5 to 0.5
- y_taps: bfloat16 [8, 2, 8, 65], P('src'), may hold values from -0.1875 to 0.1875
- source_weight: float32 [8], P('src'), may hold values from 0.0125 to 0.125
Outputs:
- intensity: float32 [4, 64, 512], P(('group', 'tile'), 'src'), parts along dimension 0
There are 2 independent parts, one for each index of `group`. A program takes and returns all parts, laid end to end along the dimension named above; an argument that names none is the same for every part. Nothing has to cross between parts.
All inputs are finite; a program needn't handle non-finite values.
Results may differ from a plain program's by a relative error of at most 0.00054.
Values may be sent and summed in bfloat16 or wider, within the bound.
No kernel may reach another device: no remote copies, remote signals or barrier semaphores. Data moves between devices by JAX's collectives and lax.ppermute only.
A program may use at most 128 MiB of HBM per device.

v0:
```python
import jax
import jax.numpy as jnp
from jax import lax
from jax.sharding import PartitionSpec as P


def padded_2(cells, sides, width):
    for axis, dim in sides:
        count = lax.axis_size(axis)
        ends = count - 1
        head = lax.slice_in_dim(cells, 0, width, axis=dim)
        tail = lax.slice_in_dim(cells, cells.shape[dim] - width, cells.shape[dim], axis=dim)
        cells = jnp.concatenate(
            [
                lax.ppermute(tail, axis, [(i, (i + 1) % count) for i in range(ends)]),
                cells,
                lax.ppermute(head, axis, [((i + 1) % count, i) for i in range(ends)]),
            ],
            axis=dim,
        )
    return cells


def column_mats(taps):
    tap_count = taps.shape[-1]
    shift = lax.broadcasted_iota(jnp.int32, (tap_count, 256, 128), 0)
    inner = lax.broadcasted_iota(jnp.int32, (tap_count, 256, 128), 1)
    outer = lax.broadcasted_iota(jnp.int32, (tap_count, 256, 128), 2)
    select = (inner - outer == shift).astype(jnp.float32)
    coef = jnp.einsum(
        "xprt,tqj->xpqrj", taps.astype(jnp.float32), select, precision=lax.Precision.HIGHEST
    )
    real_part, imag_part = (coef[:, 0], coef[:, 1])
    full = jnp.stack(
        [jnp.stack([real_part, imag_part], axis=2), jnp.stack([-imag_part, real_part], axis=2)],
        axis=1,
    ).astype(jnp.bfloat16)
    return (full[:, :, :128], full[:, :, 128:])


def column_pass(rows_field, lower_mat, upper_mat, rim_width):
    count_rows, _, comps, width = rows_field.shape
    padded = jnp.pad(rows_field, ((0, 0), (0, 0), (0, 0), (rim_width, 128 - rim_width)))
    pieces = padded.reshape(count_rows, 2, comps, width // 128 + 1, 128)
    result = jnp.einsum(
        "ipcbq,xpqsrj->ixsrcbj", pieces[:, :, :, :-1], lower_mat, preferred_element_type=jnp.float32
    )
    result = result + jnp.einsum(
        "ipcbq,xpqsrj->ixsrcbj", pieces[:, :, :, 1:], upper_mat, preferred_element_type=jnp.float32
    )
    sources, ranks = (lower_mat.shape[0], lower_mat.shape[4])
    return result.reshape(count_rows, sources, 2, ranks, comps, width).astype(jnp.bfloat16)


def row_matrices(taps, block_rows, rim_width):
    tap_count = taps.shape[-1]
    span = block_rows + 2 * rim_width
    shift = lax.broadcasted_iota(jnp.int32, (tap_count, block_rows, span), 0)
    out_row = lax.broadcasted_iota(jnp.int32, (tap_count, block_rows, span), 1)
    in_row = lax.broadcasted_iota(jnp.int32, (tap_count, block_rows, span), 2)
    select = (in_row - out_row == shift).astype(jnp.float32)
    coef = jnp.einsum(
        "xprt,tik->xpirk", taps.astype(jnp.float32), select, precision=lax.Precision.HIGHEST
    )
    real_part, imag_part = (coef[:, 0], coef[:, 1])
    full = jnp.stack(
        [jnp.stack([real_part, -imag_part], axis=2), jnp.stack([imag_part, real_part], axis=2)],
        axis=1,
    )
    return full.astype(jnp.bfloat16)


def per_device(near_field, x_taps, y_taps, source_weight):
    rim_width = (x_taps.shape[-1] - 1) // 2
    width = near_field.shape[-1]
    local_rows = near_field.shape[1]
    whole_tile = lax.all_gather(near_field, "src", axis=1, tiled=True)
    padded_field = padded_2(whole_tile, (("tile", 1),), rim_width)
    lower_mat, upper_mat = column_mats(x_taps)
    padded_pass = column_pass(padded_field[0], lower_mat, upper_mat, rim_width)
    tile_rows = padded_pass.shape[0] - 2 * rim_width
    block_rows = 64
    row_mats = row_matrices(y_taps, block_rows, rim_width)

    def one_block(index):
        first_row = index * block_rows
        window = lax.dynamic_slice_in_dim(padded_pass, first_row, block_rows + 2 * rim_width, 0)
        image = jnp.einsum(
            "xoiprk,kxprcw->xoicw", row_mats, window, preferred_element_type=jnp.float32
        )
        power = jnp.sum(image * image, axis=(1, 3))
        return jnp.sum(source_weight[:, None, None] * power, axis=0)

    blocks = lax.map(one_block, jnp.arange(tile_rows // block_rows, dtype=jnp.int32))
    own_image = blocks.reshape(tile_rows, width)
    summed = lax.psum_scatter(own_image, "src", scatter_dimension=0, tiled=True)
    return summed.reshape(1, local_rows, width)


def solution(mesh):
    placed = (
        P(("group", "tile"), "src", None, None, None),
        P("src", None, None, None),
        P("src", None, None, None),
        P("src"),
    )
    return jax.shard_map(
        per_device,
        mesh=mesh,
        in_specs=placed,
        out_specs=P(("group", "tile"), "src", None),
        check_vma=False,
    )
```

profile of v0, /device:TPU:0, one launch (start us, length us, event | category | flops | bytes accessed | tf_op | source)
XLA Modules:
  0.0 142.8 jit_solution(395169081686979123)
XLA Ops:
  6.5 33.1 %all_gather.3 = bf16[1,64,2,3,512]{4,2,3,0,1:T(2,128)(2,1)S(1)} all-gather(bf16[1,8,2,3,512]{4,2,3,0,1:T(2,128)(2,1)} %bitcast.120), channel_id=1, replica_groups=mesh['group'=2,'src'=8,'tile'=2] {'src'}, dimensions={1}, use_global_device_ids=true | all-gather | bytes 442368 | tf_op jit(solution)/shard_map/all_gather | solution.py:77
  39.6 0.3 fusion.45
  39.9 0.7 copy.29
  40.6 2.0 %collective-permute-start = (bf16[1,32,2,3,512]{4,1,3,2,0:T(8,128)(2,1)}, bf16[1,32,2,3,512]{4,1,3,2,0:T(8,128)(2,1)}, u32[]{:S(2)}, u32[]{:S(2)}) collective-permute-start(bf16[1,32,2,3,512]{4,1,3,2,0:T(8,128)(2,1)} %copy.29), channel_id=1, source_target_pairs={{0,1},{2,3},{4,5},{6,7},{8,9},{10,11},{12,13},{14,15},{16,17},{18,... | collective-permute-start | bytes 589832 | tf_op jit(solution)/shard_map/ppermute | solution.py:15
  42.6 0.7 copy.30
  43.3 1.3 collective-permute-start.1
  44.6 1.1 fusion.9
  45.9 0.5 copy-done.2
  46.4 0.5 fusion.18
  47.0 1.1 maximum_bitcast_fusion.1
  48.1 0.8 maximum_bitcast_fusion.3
  49.0 1.3 copy.32
  50.9 1.4 fusion.26
  52.3 2.2 %copy.31 = bf16[1,32,2,3,512]{1,4,3,2,0:T(8,128)(2,1)} copy(bf16[1,32,2,3,512]{4,1,3,2,0:T(8,128)(2,1)} %collective-permute-done) | data formatting | bytes 393216 | tf_op jit(solution)/shard_map/ppermute | solution.py:15
  54.5 2.1 %copy.33 = bf16[1,32,2,3,512]{1,4,3,2,0:T(8,128)(2,1)} copy(bf16[1,32,2,3,512]{4,1,3,2,0:T(8,128)(2,1)} %collective-permute-done.1) | data formatting | bytes 393216 | tf_op jit(solution)/shard_map/ppermute | solution.py:17
  56.6 2.1 %maximum_bitcast_fusion.2 = bf16[128,2,3,512]{0,3,2,1:T(8,128)(2,1)S(1)} fusion(bf16[1,32,2,3,512]{1,4,3,2,0:T(8,128)(2,1)} %copy.33, bf16[1,64,2,3,512]{1,4,3,2,0:T(8,128)(2,1)S(1)} %copy-done.1, bf16[1,32,2,3,512]{1,4,3,2,0:T(8,128)(2,1)} %copy.31), kind=kLoop, calls=%fused_computation.31 | loop fusion | flops 2359296 | bytes 1572864 | tf_op jit(solution)/shard_map/squeeze | solution.py:80
  58.8 1.1 fusion.44
  59.9 1.2 copy.61
  61.1 1.5 %copy.62 = bf16[128,2,3,4,128]{4,0,1,3,2:T(8,128)(2,1)S(1)} copy(bf16[128,2,3,4,128]{0,4,3,2,1:T(8,128)(2,1)} %get-tuple-element.24) | data formatting | bytes 1572864
  62.6 3.0 %fusion.29 = f32[2,8,128,128,3,4,1]{3,2,6,5,4,1,0:T(8,128)S(1)} fusion(bf16[2,128,2,8,128,1,1]{4,3,1,2,0,6,5:T(8,128)(2,1)S(1)} %get-tuple-element.14, bf16[128,2,3,4,128]{4,0,1,3,2:T(8,128)(2,1)} %copy.61), kind=kOutput, calls=%fused_computation.26 | convolution fusion | flops 1610612736 | bytes 14417920 | tf_op jit(solution)/shard_map/ipcbq,xpqsrj->ixsrcbj/dot_general | solution.py:45
  65.6 2.3 %fusion = bf16[2,8,128,128,3,4]{3,2,5,4,1,0:T(8,128)(2,1)S(1)} fusion(f32[2,8,128,128,3,4,1]{3,2,6,5,4,1,0:T(8,128)S(1)} %fusion.29, bf16[2,128,2,8,128,1,1]{4,3,1,2,0,6,5:T(8,128)(2,1)S(1)} %get-tuple-element.13, bf16[128,2,3,4,128]{4,0,1,3,2:T(8,128)(2,1)S(1)} %copy.62), kind=kOutput, calls=%fused_computation.1 | convolution fusion | flops 1616904192 | bytes 20709376 | tf_op jit(solution)/shard_map/ipcbq,xpqsrj->ixsrcbj/dot_general | solution.py:48
  67.9 3.2 %fusion.21 = f32[64,512]{1,0:T(8,128)S(1)} fusion(bf16[128,2,8,3,512,1]{0,4,3,2,1,5:T(8,128)(2,1)S(1)} %bitcast.119, bf16[2,64,2,8,128,1]{4,3,1,2,0,5:T(8,128)(2,1)} %maximum_bitcast_fusion.3), kind=kOutput, calls=%fused_computation.16 | convolution fusion | flops 805666816 | bytes 6946816 | tf_op jit(solution)/shard_map/while/body/eval_jaxpr/xoiprk,kxprcw->xoicw/dot_general | solution.py:88
  71.1 0.7 broadcast_multiply_fusion
  71.8 64.1 %reduce-scatter.2.cloned.1.call-done = f32[8,512]{1,0:T(8,128)} async-done(((f32[64,512]{1,0:T(8,128)}), f32[8,512]{1,0:T(8,128)}) %reduce-scatter.2.cloned.1.call-update) | async-done | bytes 16400 | tf_op jit(solution)/shard_map/reduce_scatter | solution.py:96
  (14 shorter events, 0.4 us)
Async XLA Ops:
  6.5 38.0 %copy-start = (bf16[1,2,8,65]{3,2,1,0:T(8,128)(2,1)S(1)}, bf16[1,2,8,65]{3,2,1,0:T(8,128)(2,1)}, u32[]{:S(2)}) copy-start(bf16[1,2,8,65]{3,2,1,0:T(8,128)(2,1)} %param.5) | copy-start | bytes 6244
  6.5 129.4 %reduce-scatter.2.cloned.1.call-start = ((), (), s32[]{:S(2)}) async-start(), calls=%async_computation.1 | async-start | bytes 147456 | tf_op jit(solution)/shard_map/reduce_scatter | solution.py:96
  40.6 11.8 %collective-permute-start = (bf16[1,32,2,3,512]{4,1,3,2,0:T(8,128)(2,1)}, bf16[1,32,2,3,512]{4,1,3,2,0:T(8,128)(2,1)}, u32[]{:S(2)}, u32[]{:S(2)}) collective-permute-start(bf16[1,32,2,3,512]{4,1,3,2,0:T(8,128)(2,1)} %copy.29), channel_id=1, source_target_pairs={{0,1},{2,3},{4,5},{6,7},{8,9},{10,11},{12,13},{14,15},{16,17},{18,... | collective-permute-start | bytes 589832 | tf_op jit(solution)/shard_map/ppermute | solution.py:15
  43.3 11.2 %collective-permute-start.1 = (bf16[1,32,2,3,512]{4,1,3,2,0:T(8,128)(2,1)}, bf16[1,32,2,3,512]{4,1,3,2,0:T(8,128)(2,1)}, u32[]{:S(2)}, u32[]{:S(2)}) collective-permute-start(bf16[1,32,2,3,512]{4,1,3,2,0:T(8,128)(2,1)} %copy.30), channel_id=1, source_target_pairs={{1,0},{3,2},{5,4},{7,6},{9,8},{11,10},{13,12},{15,14},{17,16},{19,... | collective-permute-start | bytes 589832 | tf_op jit(solution)/shard_map/ppermute | solution.py:17
  45.7 0.7 copy-start.2
  52.3 4.3 %copy-start.1 = (bf16[1,64,2,3,512]{1,4,3,2,0:T(8,128)(2,1)S(1)}, bf16[1,64,2,3,512]{1,4,3,2,0:T(8,128)(2,1)}, u32[]{:S(2)}) copy-start(bf16[1,64,2,3,512]{1,4,3,2,0:T(8,128)(2,1)} %copy.32) | copy-start | bytes 1179652
Sparse Core Ops, SparseCore 0:
  71.9 63.9 reduce-scatter.1
where the time goes:
time: 143 us
  waiting for transfers between devices  64.1 us (45%)
  blocking collectives  33.1 us (23%)
  between operations  14.2 us (10%)
  local copies, waits for them, and re-layouts  11.8 us (8%)
  matrix products  10.1 us (7%)
  other arithmetic  6.23 us (4%)
  starting transfers between devices  3.26 us (2%)
    reduce_scatter x1, waiting for transfers between devices, per_device(): summed = lax.psum_scatter(own_image, 'src', scatter_dimension=0, tiled=True)  64.1 us
    all_gather x1, blocking collectives, per_device(): whole_tile = lax.all_gather(near_field, 'src', axis=1, tiled=True)  33.1 us
    dot_general x1, matrix products, one_block(): jnp.einsum('xoiprk,kxprcw->xoicw', row_mats, window, preferred_element_ty...  3.22 us
    unnamed x8, local copies, waits for them, and re-layouts  3.17 us
    dot_general x1, matrix products, column_pass(): jnp.einsum('ipcbq,xpqsrj->ixsrcbj', pieces[:, :, :, :-1], lower_mat, pref...  2.99 us
  transfers between devices with their start and end apart: 3, of which 1 were waited for; matrix products, arithmetic and copies ran while one was open for 7% of the time, Pallas kernels for 0%

commit v1 on v0

--- a/solution.py
+++ b/solution.py
@@ -74,7 +74,11 @@
     rim_width = (x_taps.shape[-1] - 1) // 2
     width = near_field.shape[-1]
     local_rows = near_field.shape[1]
-    whole_tile = lax.all_gather(near_field, "src", axis=1, tiled=True)
+    count = lax.axis_size("src")
+    spread = jnp.broadcast_to(near_field, (count,) + near_field.shape[1:])
+    whole_tile = lax.all_to_all(spread, "src", 0, 0).reshape(
+        (1, count * local_rows) + near_field.shape[2:]
+    )
     padded_field = padded_2(whole_tile, (("tile", 1),), rim_width)
     lower_mat, upper_mat = column_mats(x_taps)
     padded_pass = column_pass(padded_field[0], lower_mat, upper_mat, rim_width)
@@ -93,7 +97,8 @@
 
     blocks = lax.map(one_block, jnp.arange(tile_rows // block_rows, dtype=jnp.int32))
     own_image = blocks.reshape(tile_rows, width)
-    summed = lax.psum_scatter(own_image, "src", scatter_dimension=0, tiled=True)
+    pieces = own_image.reshape(count, local_rows, width)
+    summed = jnp.sum(lax.all_to_all(pieces, "src", 0, 0), axis=0)
     return summed.reshape(1, local_rows, width)
 
 

time: 143 us -> 50.1 us (0.35)
  waiting for transfers between devices: 64.1 us -> 9.1 us
  blocking collectives: 33.1 us -> 12 us
  between operations: 14.2 us -> 0.81 us
  local copies, waits for them, and re-layouts: 11.8 us -> 4.73 us
  starting transfers between devices: 3.26 us -> 9.87 us
  other arithmetic: 6.23 us -> 2.98 us
    reduce_scatter x1 -> x0, waiting for transfers between devices: 64.1 us -> none  [per_device(): summed = lax.psum_scatter(own_image, 'src', scatter_dimension=0, tiled=True)]
    all_gather x1 -> x0, blocking collectives: 33.1 us -> none  [per_device(): whole_tile = lax.all_gather(near_field, 'src', axis=1, tiled=True)]
    all_to_all x0 -> x1, blocking collectives: none -> 12 us  [per_device(): summed = jnp.sum(lax.all_to_all(pieces, 'src', 0, 0), axis=0)]
    all_to_all x0 -> x1, waiting for transfers between devices: none -> 9.1 us  [per_device(): lax.all_to_all(spread, 'src', 0, 0)]
    all_to_all x0 -> x1, starting transfers between devices: none -> 7.28 us  [per_device(): lax.all_to_all(spread, 'src', 0, 0)]
    ppermute x2 -> x0, local copies, waits for them, and re-layouts: 4.26 us -> none  [the longest x1 2.16 us: padded_2(): lax.ppermute(tail, axis, [(i, (i + 1) % count) for i in range(ends)])]
    squeeze x1, other arithmetic: 2.09 us -> 0.08 us  [per_device(): padded_pass = column_pass(padded_field[0], lower_mat, upper_mat, rim_width)]
    broadcast_in_dim x0 -> x2, local copies, waits for them, and re-layouts: none -> 1.6 us  [per_device(): spread = jnp.broadcast_to(near_field, (count,) + near_field.shape[1:])]
  transfers between devices with their start and end apart: 3 -> 3, of which waited for: 1 -> 1; matrix products, arithmetic and copies ran while one was open for 7% -> 8% of each run, Pallas kernels for 0% -> 0%
where the time goes in v1:
time: 50.1 us; the launch traced here: 49.6 us
  blocking collectives  12 us (24%)
  matrix products  10.2 us (20%)
  starting transfers between devices  9.87 us (20%)
  waiting for transfers between devices  9.1 us (18%)
  local copies, waits for them, and re-layouts  4.73 us (9%)
  other arithmetic  2.98 us (6%)
  between operations  0.81 us (2%)
    all_to_all x1, blocking collectives, per_device(): summed = jnp.sum(lax.all_to_all(pieces, 'src', 0, 0), axis=0)  12 us
    all_to_all x1, waiting for transfers between devices, per_device(): lax.all_to_all(spread, 'src', 0, 0)  9.1 us
    all_to_all x1, starting transfers between devices, per_device(): lax.all_to_all(spread, 'src', 0, 0)  7.28 us
    dot_general x1, matrix products, one_block(): jnp.einsum('xoiprk,kxprcw->xoicw', row_mats, window, preferred_element_ty...  3.21 us
    dot_general x1, matrix products, column_pass(): jnp.einsum('ipcbq,xpqsrj->ixsrcbj', pieces[:, :, :, :-1], lower_mat, pref...  3.07 us
    unnamed x9, local copies, waits for them, and re-layouts  2.5 us
    dot_general x1, matrix products, column_pass(): jnp.einsum('ipcbq,xpqsrj->ixsrcbj', pieces[:, :, :, 1:], upper_mat, prefe...  2.26 us
    broadcast_in_dim x2, local copies, waits for them, and re-layouts, per_device(): spread = jnp.broadcast_to(near_field, (count,) + near_field.shape[1:])  1.6 us
  transfers between devices with their start and end apart: 3, of which 1 were waited for; matrix products, arithmetic and copies ran while one was open for 8% of the time, Pallas kernels for 0%

profile of v1, /device:TPU:0, one launch (start us, length us, event | category | flops | bytes accessed | tf_op | source)
XLA Modules:
  0.0 49.6 jit_solution(10396789960073704547)
XLA Ops:
  0.0 0.8 %copy.54 = bf16[8,2,3,512]{3,0,2,1:T(8,128)(2,1)S(1)} copy(bf16[8,2,3,512]{3,1,2,0:T(2,128)(2,1)} %bitcast.127) | data formatting | bytes 98304 | tf_op jit(solution)/shard_map/broadcast_in_dim | solution.py:78
  0.8 0.8 %broadcast_in_dim.14 = bf16[8,8,2,3,512]{4,1,3,2,0:T(8,128)(2,1)} broadcast(bf16[8,2,3,512]{3,0,2,1:T(8,128)(2,1)S(1)} %copy.54), dimensions={1,2,3,4} | broadcast | bytes 442368 | tf_op jit(solution)/shard_map/broadcast_in_dim | solution.py:78
  1.6 7.3 %all-to-all-start = ((bf16[8,8,2,3,512]{4,1,3,2,0:T(8,128)(2,1)}), bf16[8,8,2,3,512]{4,1,3,2,0:T(8,128)(2,1)S(1)}, u32[]{:S(2)}, u32[]{:S(2)}) async-start(bf16[8,8,2,3,512]{4,1,3,2,0:T(8,128)(2,1)} %broadcast_in_dim.14), calls=%async_computation | async-start | bytes 786432 | tf_op jit(solution)/shard_map/all_to_all | solution.py:79
  8.9 1.1 %fusion.9 = f32[1,2,256,8,128]{4,3,1,2,0:T(8,128)S(1)} fusion(bf16[1,2,8,65]{3,2,1,0:T(8,128)(2,1)S(1)} %copy-done), kind=kOutput, calls=%fused_computation.12 | convolution fusion | flops 72417280 | bytes 2099232 | tf_op jit(solution)/shard_map/xprt,tqj->xpqrj/dot_general | solution.py:30
  10.0 0.1 fusion.36
  10.3 0.5 copy-done.2
  10.7 0.5 fusion.18
  11.2 0.2 maximum_bitcast_fusion.1
  11.5 9.1 %all-to-all-done = bf16[8,8,2,3,512]{4,1,3,2,0:T(8,128)(2,1)S(1)} async-done(((bf16[8,8,2,3,512]{4,1,3,2,0:T(8,128)(2,1)}), bf16[8,8,2,3,512]{4,1,3,2,0:T(8,128)(2,1)S(1)}, u32[]{:S(2)}, u32[]{:S(2)}) %all-to-all-start) | async-done | bytes 393248 | tf_op jit(solution)/shard_map/all_to_all | solution.py:79
  20.6 1.3 %collective-permute-start = (bf16[1,32,2,3,512]{4,1,3,2,0:T(8,128)(2,1)S(1)}, bf16[1,32,2,3,512]{4,1,3,2,0:T(8,128)(2,1)S(1)}, u32[]{:S(2)}, u32[]{:S(2)}) collective-permute-start(bf16[1,32,2,3,512]{4,1,3,2,0:T(8,128)(2,1)S(1)} %get-tuple-element.30), channel_id=1, source_target_pairs={{0,1},{2,3},{4,5},{6,7},{8,9},{10,11},{12,13},{14,15},{16,17},{18,... | collective-permute-start | bytes 589832 | tf_op jit(solution)/shard_map/ppermute | solution.py:15
  22.0 1.3 %collective-permute-start.1 = (bf16[1,32,2,3,512]{4,1,3,2,0:T(8,128)(2,1)S(1)}, bf16[1,32,2,3,512]{4,1,3,2,0:T(8,128)(2,1)S(1)}, u32[]{:S(2)}, u32[]{:S(2)}) collective-permute-start(bf16[1,32,2,3,512]{4,1,3,2,0:T(8,128)(2,1)S(1)} %get-tuple-element.31), channel_id=1, source_target_pairs={{1,0},{3,2},{5,4},{7,6},{9,8},{11,10},{13,12},{15,14},{17,16},{19,... | collective-permute-start | bytes 589832 | tf_op jit(solution)/shard_map/ppermute | solution.py:17
  23.3 0.9 %maximum_bitcast_fusion.3 = bf16[2,64,2,8,128,1]{4,3,1,2,0,5:T(8,128)(2,1)} fusion(bf16[1,64,1,8,128]{4,3,1,2,0:T(8,128)(2,1)S(1)} %get-tuple-element.27, bf16[1,64,1,8,128]{4,3,1,2,0:T(8,128)(2,1)S(1)} %get-tuple-element.26, bf16[1,64,1,8,128]{4,3,1,2,0:T(8,128)(2,1)S(1)} %fusion.39), kind=kLoop, calls=%fused_computation.37 | loop fusion | flops 786432 | bytes 917504 | tf_op jit(solution)/shard_map/stack | solution.py:66
  24.8 1.1 %fusion.26 = (bf16[2,128,2,8,128,1,1]{4,3,1,2,0,6,5:T(8,128)(2,1)}, bf16[2,128,2,8,128,1,1]{4,3,1,2,0,6,5:T(8,128)(2,1)S(1)}) fusion(bf16[1,1,256,2,8,128]{5,4,2,3,1,0:T(8,128)(2,1)S(1)} %get-tuple-element.28, bf16[1,1,256,2,8,128]{5,4,2,3,1,0:T(8,128)(2,1)S(1)} %get-tuple-element.29), kind=kLoop, calls=%fused_computation.20 | loop fusion | flops 1048576 | bytes 4194304 | tf_op jit(solution)/shard_map/reshape.11
  25.9 0.1 maximum_bitcast_fusion.2
  26.0 0.4 copy.86
  26.4 0.1 pad.4.clone
  26.5 0.3 fusion.44
  26.8 1.2 %copy.84 = bf16[128,2,3,4,128]{4,0,1,3,2:T(8,128)(2,1)} copy(bf16[128,2,3,4,128]{0,4,3,2,1:T(8,128)(2,1)S(1)} %get-tuple-element.25) | data formatting | bytes 1572864
  28.0 0.4 copy.85
  28.5 3.1 %fusion.29 = f32[2,8,128,128,3,4,1]{3,2,6,5,4,1,0:T(8,128)S(1)} fusion(bf16[2,128,2,8,128,1,1]{4,3,1,2,0,6,5:T(8,128)(2,1)S(1)} %get-tuple-element.14, bf16[128,2,3,4,128]{4,0,1,3,2:T(8,128)(2,1)} %copy.84), kind=kOutput, calls=%fused_computation.26 | convolution fusion | flops 1610612736 | bytes 14417920 | tf_op jit(solution)/shard_map/ipcbq,xpqsrj->ixsrcbj/dot_general | solution.py:45
  31.6 2.3 %fusion = bf16[2,8,128,128,3,4]{3,2,5,4,1,0:T(8,128)(2,1)S(1)} fusion(f32[2,8,128,128,3,4,1]{3,2,6,5,4,1,0:T(8,128)S(1)} %fusion.29, bf16[2,128,2,8,128,1,1]{4,3,1,2,0,6,5:T(8,128)(2,1)S(1)} %copy-done.1, bf16[128,2,3,4,128]{4,0,1,3,2:T(8,128)(2,1)S(1)} %copy.85), kind=kOutput, calls=%fused_computation.1 | convolution fusion | flops 1616904192 | bytes 20709376 | tf_op jit(solution)/shard_map/ipcbq,xpqsrj->ixsrcbj/dot_general | solution.py:48
  33.8 3.2 %fusion.21 = f32[64,512]{1,0:T(8,128)S(1)} fusion(bf16[128,2,8,3,512,1]{0,4,3,2,1,5:T(8,128)(2,1)S(1)} %bitcast.124, bf16[2,64,2,8,128,1]{4,3,1,2,0,5:T(8,128)(2,1)} %maximum_bitcast_fusion.3), kind=kOutput, calls=%fused_computation.16 | convolution fusion | flops 805666816 | bytes 6946816 | tf_op jit(solution)/shard_map/while/body/eval_jaxpr/xoiprk,kxprcw->xoicw/dot_general | solution.py:92
  37.1 12.0 %all_to_all.10 = f32[8,8,512]{2,1,0:T(8,128)S(1)} all-to-all(f32[8,8,512]{2,1,0:T(8,128)S(1)} %multiply_bitcast_fusion), channel_id=1, replica_groups=mesh['group'=2,'src'=8,'tile'=2] {'src'}, dimensions={0} | all-to-all | bytes 262144 | tf_op jit(solution)/shard_map/all_to_all | solution.py:101
  49.0 0.6 %reduce_sum.25 = f32[8,512]{1,0:T(8,128)} reduce(f32[8,8,512]{2,1,0:T(8,128)S(1)} %all_to_all.10, f32[]{:T(128)} %constant.9.clone.1), dimensions={0}, to_apply=%region_1.2 | reduce | flops 28672 | bytes 147460 | tf_op jit(solution)/shard_map/reduce_sum | solution.py:101
  (13 shorter events, 0.2 us)
Async XLA Ops:
  0.0 8.9 %copy-start = (bf16[1,2,8,65]{3,2,1,0:T(8,128)(2,1)S(1)}, bf16[1,2,8,65]{3,2,1,0:T(8,128)(2,1)}, u32[]{:S(2)}) copy-start(bf16[1,2,8,65]{3,2,1,0:T(8,128)(2,1)} %param.5) | copy-start | bytes 6244
  1.6 19.0 %all-to-all-start = ((bf16[8,8,2,3,512]{4,1,3,2,0:T(8,128)(2,1)}), bf16[8,8,2,3,512]{4,1,3,2,0:T(8,128)(2,1)S(1)}, u32[]{:S(2)}, u32[]{:S(2)}) async-start(bf16[8,8,2,3,512]{4,1,3,2,0:T(8,128)(2,1)} %broadcast_in_dim.14), calls=%async_computation | async-start | bytes 786432 | tf_op jit(solution)/shard_map/all_to_all | solution.py:79
  10.0 0.7 %copy-start.2 = (bf16[1,2,8,65]{3,2,1,0:T(8,128)(2,1)S(1)}, bf16[1,2,8,65]{3,2,1,0:T(8,128)(2,1)}, u32[]{:S(2)}) copy-start(bf16[1,2,8,65]{3,2,1,0:T(8,128)(2,1)} %param.6) | copy-start | bytes 6244
  20.6 5.3 %collective-permute-start = (bf16[1,32,2,3,512]{4,1,3,2,0:T(8,128)(2,1)S(1)}, bf16[1,32,2,3,512]{4,1,3,2,0:T(8,128)(2,1)S(1)}, u32[]{:S(2)}, u32[]{:S(2)}) collective-permute-start(bf16[1,32,2,3,512]{4,1,3,2,0:T(8,128)(2,1)S(1)} %get-tuple-element.30), channel_id=1, source_target_pairs={{0,1},{2,3},{4,5},{6,7},{8,9},{10,11},{12,13},{14,15},{16,17},{18,... | collective-permute-start | bytes 589832 | tf_op jit(solution)/shard_map/ppermute | solution.py:15
  22.0 4.0 %collective-permute-start.1 = (bf16[1,32,2,3,512]{4,1,3,2,0:T(8,128)(2,1)S(1)}, bf16[1,32,2,3,512]{4,1,3,2,0:T(8,128)(2,1)S(1)}, u32[]{:S(2)}, u32[]{:S(2)}) collective-permute-start(bf16[1,32,2,3,512]{4,1,3,2,0:T(8,128)(2,1)S(1)} %get-tuple-element.31), channel_id=1, source_target_pairs={{1,0},{3,2},{5,4},{7,6},{9,8},{11,10},{13,12},{15,14},{17,16},{19,... | collective-permute-start | bytes 589832 | tf_op jit(solution)/shard_map/ppermute | solution.py:17
  28.5 3.1 %copy-start.1 = (bf16[2,128,2,8,128,1,1]{4,3,1,2,0,6,5:T(8,128)(2,1)S(1)}, bf16[2,128,2,8,128,1,1]{4,3,1,2,0,6,5:T(8,128)(2,1)}, u32[]{:S(2)}) copy-start(bf16[2,128,2,8,128,1,1]{4,3,1,2,0,6,5:T(8,128)(2,1)} %get-tuple-element.13) | copy-start | bytes 3145732

commit v2 on v0

v2 whole, which is shorter than its diff:
```python
import functools

import jax
import jax.numpy as jnp
from jax import lax
from jax.experimental import pallas as pl
from jax.experimental.pallas import tpu as pltpu
from jax.sharding import PartitionSpec as P

LANES = 128
F32 = jnp.float32
BF16 = jnp.bfloat16


def send_kernel(rim, field_ref, x_taps_ref, y_taps_ref, weight_ref, send_ref):
    _, rows, comps, _, width = field_ref.shape
    sources, tiles, height, lanes = send_ref.shape
    ranks, taps = x_taps_ref.shape[2:]
    mine = width // (sources * tiles)
    window = mine + 2 * rim
    edge = jnp.zeros((rows, rim), F32)
    field = field_ref[0].astype(F32)
    padded = [
        [jnp.concatenate([edge, field[:, comp, part, :], edge], axis=1) for part in range(2)] for comp in range(comps)
    ]
    lines = [ref[0, part].astype(F32) for ref in (x_taps_ref, y_taps_ref) for part in range(2)]
    weight = jnp.full((ranks, 1), weight_ref[0], F32)
    high = weight.astype(BF16).astype(F32)
    middle = (weight - high).astype(BF16).astype(F32)
    low = weight - high - middle
    spare = [line[:, taps - 1 :] for line in lines] + [high, middle, low]
    spare.append(jnp.zeros((ranks, lanes - 2 * window - len(spare)), F32))
    spare = jnp.concatenate(spare, axis=1)
    spare = jnp.concatenate([spare, jnp.zeros((comps * rows - ranks, spare.shape[1]), F32)], axis=0)
    held = jnp.concatenate([line[:, : taps - 1] for line in lines], axis=1)
    for device in range(sources * tiles):
        at = device * mine
        cells = [jnp.concatenate([plane[:, at : at + window] for plane in padded[comp]], axis=1) for comp in range(comps)]
        cells = jnp.concatenate([jnp.concatenate(cells, axis=0), spare], axis=1)
        source, tile = divmod(device, tiles)
        send_ref[source, tile] = jnp.concatenate([cells, held], axis=0).astype(BF16)


def rolled(line, count):
    return pltpu.roll(jnp.broadcast_to(line, (count, line.shape[1])), 0, 1, stride=1, stride_axis=0)


def image_kernel(rim, comps, rows, ranks, got_ref, out_ref, field_ref, lhs_ref, row_ref, total_ref):
    sources, tiles, _, lanes = got_ref.shape
    mine, slab_rows = total_ref.shape
    window = mine + 2 * rim
    tile_rows = sources * rows
    chunks = slab_rows // LANES
    windows = row_ref.shape[1]
    half_lanes = LANES // 2
    for tile in range(tiles):
        cells = got_ref[:, tile].astype(F32)
        for comp in range(comps):
            some = cells[:, comp * rows : (comp + 1) * rows, :].reshape(tile_rows, lanes).astype(BF16)
            at = comp * slab_rows + tile * tile_rows
            field_ref[at : at + tile_rows, :] = some

    tap = lax.broadcasted_iota(jnp.int32, (2 * rim, lanes), 0)
    lane = lax.broadcasted_iota(jnp.int32, (2 * rim, lanes), 1)
    re_place = (lane == tap).astype(BF16)
    im_place = (lane == tap + window).astype(BF16)
    y_place = (lane == (rim - tap) % LANES).astype(BF16)[:, :LANES]
    one = lane[:1]
    re_last = (one == 2 * rim).astype(F32)
    im_last = (one == 2 * rim + window).astype(F32)
    y_last = (one == LANES - rim).astype(F32)[:, :LANES]
    k = lax.broadcasted_iota(jnp.int32, (LANES, LANES), 0)
    i = lax.broadcasted_iota(jnp.int32, (LANES, LANES), 1)
    near = jnp.abs(i - k) < half_lanes
    masks = [near] if windows == 1 else [k - i > half_lanes, near, k - i < -half_lanes]
    total_ref[...] = jnp.zeros_like(total_ref)

    def placed(first, last, place, last_place):
        return jnp.dot(first, place, preferred_element_type=F32) + last * last_place

    def one_source(source, slot):
        block = got_ref[source, 0].astype(F32)
        held = block[comps * rows : comps * rows + ranks]
        firsts = [held[:, 2 * rim * n : 2 * rim * (n + 1)].astype(BF16) for n in range(4)]
        spare = block[:ranks, 2 * window :]
        lasts = [spare[:, n : n + 1] for n in range(4)]
        weight = spare[:1, 4:5] + spare[:1, 5:6] + spare[:1, 6:7]
        at_re = [placed(firsts[n], lasts[n], re_place, re_last) for n in range(2)]
        at_im = [placed(firsts[n], lasts[n], im_place, im_last) for n in range(2)]
        x_lines = [at_re[0] - at_im[1], at_re[1] + at_im[0]]
        y_lines = [placed(firsts[n], lasts[n], y_place, y_last) for n in range(2, 4)]
        column_mat = jnp.concatenate(
            [rolled(x_lines[out][r : r + 1], mine) for r in range(ranks) for out in range(2)], axis=0
        ).astype(BF16)
        passed = lax.dot_general(column_mat, field_ref[...], (((1,), (1,)), ((), ())), preferred_element_type=F32)
        for chunk in range(chunks):
            for n in range(2 * ranks):
                cells = [
                    passed[n * mine : (n + 1) * mine, comp * slab_rows + chunk * LANES : comp * slab_rows + (chunk + 1) * LANES]
                    for comp in range(comps)
                ]
                lhs_ref[slot, chunk, :, n * LANES : (n + 1) * LANES] = jnp.concatenate(cells, axis=0).astype(BF16)
        for r in range(ranks):
            re, im = (rolled(lines[r : r + 1], LANES) for lines in y_lines)
            at = 2 * r * LANES
            for n, mask in enumerate(masks):
                re_n, im_n = jnp.where(mask, re, 0.0), jnp.where(mask, im, 0.0)
                row_ref[slot, n, at : at + LANES, :LANES] = re_n.astype(BF16)
                row_ref[slot, n, at : at + LANES, LANES:] = im_n.astype(BF16)
                row_ref[slot, n, at + LANES : at + 2 * LANES, :LANES] = (-im_n).astype(BF16)
                row_ref[slot, n, at + LANES : at + 2 * LANES, LANES:] = re_n.astype(BF16)
        for chunk in range(chunks):
            image = None
            for n in range(windows):
                other = chunk + n - windows // 2
                if 0 <= other < chunks:
                    term = jnp.dot(lhs_ref[slot, other], row_ref[slot, n], preferred_element_type=F32)
                    image = term if image is None else image + term
            square = image * image
            square = square[:, :LANES] + square[:, LANES:]
            power = square[:mine]
            for comp in range(1, comps):
                power = power + square[comp * mine : (comp + 1) * mine]
            total_ref[:, chunk * LANES : (chunk + 1) * LANES] += weight * power

    if sources <= 8:
        for source in range(sources):
            one_source(source, source % 2)
    else:
        lax.fori_loop(0, sources, lambda source, _: one_source(source, 0), None)
    for chunk in range(chunks):
        lines = total_ref[:, chunk * LANES : (chunk + 1) * LANES].T
        for piece in range(LANES // rows):
            tile, source = divmod((chunk * LANES) // rows + piece, sources)
            out_ref[source, tile] = lines[piece * rows : (piece + 1) * rows]


def merge_kernel(parts_ref, out_ref):
    out_ref[0] = jnp.concatenate([parts_ref[n] for n in range(parts_ref.shape[0])], axis=1)


def per_device(near_field, x_taps, y_taps, source_weight):
    sources, tiles = lax.axis_size("src"), lax.axis_size("tile")
    _, rows, _, comps, width = near_field.shape
    ranks, taps = x_taps.shape[-2:]
    rim = (taps - 1) // 2
    devices = sources * tiles
    mine = width // devices
    lanes = 2 * LANES
    slab_rows = devices * rows
    chunks = slab_rows // LANES
    windows = 1 if chunks == 1 else 3
    height = comps * rows + ranks
    params = pltpu.CompilerParams(vmem_limit_bytes=48 * 1024 * 1024)
    whole = pl.BlockSpec(memory_space=pltpu.VMEM)
    send = pl.pallas_call(
        functools.partial(send_kernel, rim),
        out_shape=jax.ShapeDtypeStruct((sources, tiles, height, lanes), BF16),
        in_specs=[whole] * 3 + [pl.BlockSpec(memory_space=pltpu.SMEM)],
        out_specs=whole,
        compiler_params=params,
        name="send_columns",
    )(near_field.transpose(0, 1, 3, 2, 4), x_taps, y_taps, source_weight)
    got = lax.all_to_all(send.reshape(devices, height, lanes), ("src", "tile"), 0, 0).reshape(send.shape)
    slots = 2 if sources <= 8 else 1
    image = pl.pallas_call(
        functools.partial(image_kernel, rim, comps, rows, ranks),
        out_shape=jax.ShapeDtypeStruct((sources, tiles, rows, mine), F32),
        in_specs=[whole],
        out_specs=whole,
        scratch_shapes=[
            pltpu.VMEM((comps * slab_rows, lanes), BF16),
            pltpu.VMEM((slots, chunks, comps * mine, 2 * ranks * LANES), BF16),
            pltpu.VMEM((slots, windows, 2 * ranks * LANES, 2 * LANES), BF16),
            pltpu.VMEM((mine, slab_rows), F32),
        ],
        compiler_params=params,
        name="image",
    )(got)
    parts = lax.all_to_all(image.reshape(devices, rows, mine), ("src", "tile"), 0, 0)
    return pl.pallas_call(
        merge_kernel,
        out_shape=jax.ShapeDtypeStruct((1, rows, width), F32),
        in_specs=[whole],
        out_specs=whole,
        compiler_params=params,
        name="merge_columns",
    )(parts)


def solution(mesh):
    placed = (
        P(("group", "tile"), "src", None, None, None),
        P("src", None, None, None),
        P("src", None, None, None),
        P("src"),
    )
    return jax.shard_map(
        per_device,
        mesh=mesh,
        in_specs=placed,
        out_specs=P(("group", "tile"), "src", None),
        check_vma=False,
    )
```

time: 143 us -> 36.3 us (0.25)
  waiting for transfers between devices: 64.1 us -> 0 us
  between operations: 14.2 us -> 0.7 us
  matrix products: 10.1 us -> 0 us
  local copies, waits for them, and re-layouts: 11.8 us -> 2.85 us
  blocking collectives: 33.1 us -> 26.5 us
  other arithmetic: 6.23 us -> 0.68 us
  Pallas kernels: 0 us -> 5.23 us
  starting transfers between devices: 3.26 us -> 0 us
    reduce_scatter x1 -> x0, waiting for transfers between devices: 64.1 us -> none  [per_device(): summed = lax.psum_scatter(own_image, 'src', scatter_dimension=0, tiled=True)]
    all_gather x1 -> x0, blocking collectives: 33.1 us -> none  [per_device(): whole_tile = lax.all_gather(near_field, 'src', axis=1, tiled=True)]
    all_to_all x0 -> x2, blocking collectives: none -> 26.5 us  [the longest x1 17.2 us: per_device(): lax.all_to_all(send.reshape(devices, height, lanes), ('src', 'tile'), 0, 0)]
    dot_general x5 -> x0, matrix products: 10.1 us -> none  [the longest x1 3.22 us: one_block(): jnp.einsum('xoiprk,kxprcw->xoicw', row_mats, window, preferred_element_ty...]
    pallas_call x0 -> x3, Pallas kernels: none -> 5.23 us  [the longest x1 4.32 us: per_device(): pl.pallas_call(functools.partial(image_kernel, rim, comps, rows, ranks),...]
    ppermute x2 -> x0, local copies, waits for them, and re-layouts: 4.26 us -> none  [the longest x1 2.16 us: padded_2(): lax.ppermute(tail, axis, [(i, (i + 1) % count) for i in range(ends)])]
    another operation x5 -> x0, other arithmetic: 3.48 us -> none
    ppermute x2 -> x0, starting transfers between devices: 3.26 us -> none  [the longest x1 1.98 us: padded_2(): lax.ppermute(tail, axis, [(i, (i + 1) % count) for i in range(ends)])]
  transfers between devices with their start and end apart: 3 -> 0, of which waited for: 1 -> 0; matrix products, arithmetic and copies ran while one was open for 7% -> 0% of each run, Pallas kernels for 0% -> 0%
where the time goes in v2:
time: 36.3 us; the launch traced here: 36 us
  blocking collectives  26.5 us (73%)
  Pallas kernels  5.23 us (14%)
  local copies, waits for them, and re-layouts  2.85 us (8%)
  between operations  0.7 us (2%)
  other arithmetic  0.68 us (2%)
    all_to_all x1, blocking collectives, per_device(): lax.all_to_all(send.reshape(devices, height, lanes), ('src', 'tile'), 0, 0)  17.2 us
    all_to_all x1, blocking collectives, per_device(): lax.all_to_all(image.reshape(devices, rows, mine), ('src', 'tile'), 0, 0)  9.27 us
    pallas_call x1, Pallas kernels, per_device(): pl.pallas_call(functools.partial(image_kernel, rim, comps, rows, ranks),...  4.32 us
    unnamed x8, local copies, waits for them, and re-layouts  2.34 us

profile of v2, /device:TPU:0, one launch (start us, length us, event | category | flops | bytes accessed | tf_op | source)
XLA Modules:
  0.0 36.0 jit_solution(9909067696133492395)
XLA Ops:
  0.7 0.0 copy-start
  0.7 0.8 %copy-done = bf16[1,8,2,3,512]{4,2,3,1,0:T(2,128)(2,1)S(1)} copy-done((bf16[1,8,2,3,512]{4,2,3,1,0:T(2,128)(2,1)S(1)}, bf16[1,8,2,3,512]{4,2,3,1,0:T(2,128)(2,1)}, u32[]{:S(2)}) %copy-start) | copy-done | bytes 49176
  1.5 0.0 copy-start.1
  1.5 0.7 %copy-done.1 = bf16[1,2,8,65]{3,2,1,0:T(8,128)(2,1)S(1)} copy-done((bf16[1,2,8,65]{3,2,1,0:T(8,128)(2,1)S(1)}, bf16[1,2,8,65]{3,2,1,0:T(8,128)(2,1)}, u32[]{:S(2)}) %copy-start.1) | copy-done | bytes 2104
  2.1 0.0 copy-start.2
  2.1 0.7 %copy-done.2 = bf16[1,2,8,65]{3,2,1,0:T(8,128)(2,1)S(1)} copy-done((bf16[1,2,8,65]{3,2,1,0:T(8,128)(2,1)S(1)}, bf16[1,2,8,65]{3,2,1,0:T(8,128)(2,1)}, u32[]{:S(2)}) %copy-start.2) | copy-done | bytes 2104
  2.8 0.2 send_columns.1
  3.1 17.2 %all_to_all.10 = bf16[16,32,256]{2,1,0:T(8,128)(2,1)S(1)} all-to-all(bf16[16,32,256]{2,1,0:T(8,128)(2,1)S(1)} %bitcast.5), channel_id=1, replica_groups=mesh['group'=2,'src'=8,'tile'=2] {'src','tile'}, dimensions={0} | all-to-all | bytes 524288 | tf_op jit(solution)/shard_map/all_to_all | solution.py:164
  20.3 4.3 %image.1 = f32[8,2,8,32]{3,2,1,0:T(8,128)S(1)} custom-call(bf16[8,2,32,256]{3,2,1,0:T(8,128)(2,1)S(1)} %bitcast.4), custom_call_target="tpu_custom_call" | custom-call | tf_op jit(solution)/shard_map/image/pallas_call | solution.py:166
  24.6 0.1 reshape.12
  24.7 9.3 %all_to_all.11 = f32[16,1,256]{2,1,0:T(1,128)S(1)} all-to-all(f32[16,1,256]{2,1,0:T(1,128)S(1)} %reshape.12), channel_id=1, replica_groups=mesh['group'=2,'src'=8,'tile'=2] {'src','tile'}, dimensions={0} | all-to-all | bytes 32768 | tf_op jit(solution)/shard_map/all_to_all | solution.py:180
  34.0 0.5 %broadcast = f32[]{:T(128)} broadcast(f32[]{:T(128)} %constant.4), dimensions={} | broadcast | bytes 8 | tf_op jit(solution)/shard_map/all_to_all | solution.py:180
  34.5 0.7 %reduce = f32[16,256]{1,0:T(8,128)S(1)} reduce(f32[16,1,256]{2,1,0:T(1,128)S(1)} %all_to_all.11, f32[]{:T(128)} %broadcast), dimensions={1}, to_apply=%all_to_all.7.reduce_sub_computation | reduce | bytes 32772 | tf_op jit(solution)/shard_map/all_to_all | solution.py:180
  35.2 0.1 reshape.13.parts_ref
  35.3 0.7 %merge_columns.1 = f32[1,8,512]{2,1,0:T(8,128)} custom-call(f32[16,8,32]{2,1,0:T(8,128)S(1)} %reshape.13.parts_ref), custom_call_target="tpu_custom_call" | custom-call | tf_op jit(solution)/shard_map/merge_columns/pallas_call | solution.py:181
Async XLA Ops:
  0.7 0.8 %copy-start = (bf16[1,8,2,3,512]{4,2,3,1,0:T(2,128)(2,1)S(1)}, bf16[1,8,2,3,512]{4,2,3,1,0:T(2,128)(2,1)}, u32[]{:S(2)}) copy-start(bf16[1,8,2,3,512]{4,2,3,1,0:T(2,128)(2,1)} %param.4) | copy-start | bytes 147460
  1.5 0.7 %copy-start.1 = (bf16[1,2,8,65]{3,2,1,0:T(8,128)(2,1)S(1)}, bf16[1,2,8,65]{3,2,1,0:T(8,128)(2,1)}, u32[]{:S(2)}) copy-start(bf16[1,2,8,65]{3,2,1,0:T(8,128)(2,1)} %x_taps_ref.1) | copy-start | bytes 6244
  2.1 0.7 %copy-start.2 = (bf16[1,2,8,65]{3,2,1,0:T(8,128)(2,1)S(1)}, bf16[1,2,8,65]{3,2,1,0:T(8,128)(2,1)}, u32[]{:S(2)}) copy-start(bf16[1,2,8,65]{3,2,1,0:T(8,128)(2,1)} %y_taps_ref.1) | copy-start | bytes 6244

commit v3 on v2

--- a/solution.py
+++ b/solution.py
@@ -12,7 +12,15 @@
 BF16 = jnp.bfloat16
 
 
-def send_kernel(rim, field_ref, x_taps_ref, y_taps_ref, weight_ref, send_ref):
+def send_kernel(
+    rim, field_hbm, x_taps_hbm, y_taps_hbm, weight_ref, send_ref, field_ref, x_taps_ref, y_taps_ref, sems
+):
+    pairs = ((field_hbm, field_ref), (x_taps_hbm, x_taps_ref), (y_taps_hbm, y_taps_ref))
+    copies = [pltpu.make_async_copy(source, target, sems.at[n]) for n, (source, target) in enumerate(pairs)]
+    for copy in copies:
+        copy.start()
+    for copy in copies:
+        copy.wait()
     _, rows, comps, _, width = field_ref.shape
     sources, tiles, height, lanes = send_ref.shape
     ranks, taps = x_taps_ref.shape[2:]
@@ -23,22 +31,25 @@
     padded = [
         [jnp.concatenate([edge, field[:, comp, part, :], edge], axis=1) for part in range(2)] for comp in range(comps)
     ]
-    lines = [ref[0, part].astype(F32) for ref in (x_taps_ref, y_taps_ref) for part in range(2)]
+    lower = lax.axis_index("tile") == 0
+    lines = [
+        jnp.where(lower, x_taps_ref[0, part].astype(F32), y_taps_ref[0, part].astype(F32)) for part in range(2)
+    ]
     weight = jnp.full((ranks, 1), weight_ref[0], F32)
     high = weight.astype(BF16).astype(F32)
     middle = (weight - high).astype(BF16).astype(F32)
     low = weight - high - middle
-    spare = [line[:, taps - 1 :] for line in lines] + [high, middle, low]
-    spare.append(jnp.zeros((ranks, lanes - 2 * window - len(spare)), F32))
-    spare = jnp.concatenate(spare, axis=1)
-    spare = jnp.concatenate([spare, jnp.zeros((comps * rows - ranks, spare.shape[1]), F32)], axis=0)
-    held = jnp.concatenate([line[:, : taps - 1] for line in lines], axis=1)
+    last = [line[:, taps - 1 :] for line in lines] + [high, middle, low]
+    last.append(jnp.zeros((ranks, taps - 1 - len(last)), F32))
+    spare = jnp.concatenate([line[:, : taps - 1] for line in lines] + [jnp.concatenate(last, axis=1)], axis=0)
+    unused = lanes - 2 * window - (taps - 1)
+    if unused > 0:
+        spare = jnp.concatenate([spare, jnp.zeros((height, unused), F32)], axis=1)
     for device in range(sources * tiles):
         at = device * mine
         cells = [jnp.concatenate([plane[:, at : at + window] for plane in padded[comp]], axis=1) for comp in range(comps)]
-        cells = jnp.concatenate([jnp.concatenate(cells, axis=0), spare], axis=1)
         source, tile = divmod(device, tiles)
-        send_ref[source, tile] = jnp.concatenate([cells, held], axis=0).astype(BF16)
+        send_ref[source, tile] = jnp.concatenate([jnp.concatenate(cells, axis=0), spare], axis=1).astype(BF16)
 
 
 def rolled(line, count):
@@ -79,12 +90,11 @@
         return jnp.dot(first, place, preferred_element_type=F32) + last * last_place
 
     def one_source(source, slot):
-        block = got_ref[source, 0].astype(F32)
-        held = block[comps * rows : comps * rows + ranks]
-        firsts = [held[:, 2 * rim * n : 2 * rim * (n + 1)].astype(BF16) for n in range(4)]
-        spare = block[:ranks, 2 * window :]
-        lasts = [spare[:, n : n + 1] for n in range(4)]
-        weight = spare[:1, 4:5] + spare[:1, 5:6] + spare[:1, 6:7]
+        blocks = [got_ref[source, tile].astype(F32)[:, 2 * window : 2 * window + 2 * rim] for tile in range(2)]
+        firsts = [block[part * ranks : (part + 1) * ranks].astype(BF16) for block in blocks for part in range(2)]
+        lasts = [block[2 * ranks : 3 * ranks, part : part + 1] for block in blocks for part in range(2)]
+        weight = blocks[0][2 * ranks : 2 * ranks + 1]
+        weight = weight[:, 2:3] + weight[:, 3:4] + weight[:, 4:5]
         at_re = [placed(firsts[n], lasts[n], re_place, re_last) for n in range(2)]
         at_im = [placed(firsts[n], lasts[n], im_place, im_last) for n in range(2)]
         x_lines = [at_re[0] - at_im[1], at_re[1] + at_im[0]]
@@ -132,11 +142,21 @@
         lines = total_ref[:, chunk * LANES : (chunk + 1) * LANES].T
         for piece in range(LANES // rows):
             tile, source = divmod((chunk * LANES) // rows + piece, sources)
-            out_ref[source, tile] = lines[piece * rows : (piece + 1) * rows]
+            block = lines[piece * rows : (piece + 1) * rows]
+            step = out_ref.shape[2]
+            groups = [block[n : n + step] for n in range(0, rows, step)]
+            out_ref[source, tile] = jnp.concatenate(groups, axis=1)
 
 
 def merge_kernel(parts_ref, out_ref):
-    out_ref[0] = jnp.concatenate([parts_ref[n] for n in range(parts_ref.shape[0])], axis=1)
+    devices = parts_ref.shape[0]
+    mine = out_ref.shape[2] // devices
+    blocks = []
+    for device in range(devices):
+        part = parts_ref[device]
+        groups = [part[:, at : at + mine] for at in range(0, part.shape[1], mine)]
+        blocks.append(jnp.concatenate(groups, axis=0))
+    out_ref[0] = jnp.concatenate(blocks, axis=1)
 
 
 def per_device(near_field, x_taps, y_taps, source_weight):
@@ -150,22 +170,33 @@
     slab_rows = devices * rows
     chunks = slab_rows // LANES
     windows = 1 if chunks == 1 else 3
-    height = comps * rows + ranks
+    height = comps * rows
+    step = max(1, rows * mine // LANES)
     params = pltpu.CompilerParams(vmem_limit_bytes=48 * 1024 * 1024)
     whole = pl.BlockSpec(memory_space=pltpu.VMEM)
+
+    def in_hbm(array):
+        return pltpu.with_memory_space_constraint(array, pltpu.HBM)
+
     send = pl.pallas_call(
         functools.partial(send_kernel, rim),
         out_shape=jax.ShapeDtypeStruct((sources, tiles, height, lanes), BF16),
-        in_specs=[whole] * 3 + [pl.BlockSpec(memory_space=pltpu.SMEM)],
+        in_specs=[pl.BlockSpec(memory_space=pltpu.HBM)] * 3 + [pl.BlockSpec(memory_space=pltpu.SMEM)],
         out_specs=whole,
+        scratch_shapes=[
+            pltpu.VMEM((1, rows, comps, 2, width), BF16),
+            pltpu.VMEM(x_taps.shape, BF16),
+            pltpu.VMEM(y_taps.shape, BF16),
+            pltpu.SemaphoreType.DMA((3,)),
+        ],
         compiler_params=params,
         name="send_columns",
-    )(near_field.transpose(0, 1, 3, 2, 4), x_taps, y_taps, source_weight)
+    )(in_hbm(near_field.transpose(0, 1, 3, 2, 4)), in_hbm(x_taps), in_hbm(y_taps), source_weight)
     got = lax.all_to_all(send.reshape(devices, height, lanes), ("src", "tile"), 0, 0).reshape(send.shape)
     slots = 2 if sources <= 8 else 1
     image = pl.pallas_call(
         functools.partial(image_kernel, rim, comps, rows, ranks),
-        out_shape=jax.ShapeDtypeStruct((sources, tiles, rows, mine), F32),
+        out_shape=jax.ShapeDtypeStruct((sources, tiles, step, rows // step * mine), F32),
         in_specs=[whole],
         out_specs=whole,
         scratch_shapes=[
@@ -177,7 +208,7 @@
         compiler_params=params,
         name="image",
     )(got)
-    parts = lax.all_to_all(image.reshape(devices, rows, mine), ("src", "tile"), 0, 0)
+    parts = lax.all_to_all(image.reshape((devices,) + image.shape[2:]), ("src", "tile"), 0, 0)
     return pl.pallas_call(
         merge_kernel,
         out_shape=jax.ShapeDtypeStruct((1, rows, width), F32),

time: 36.3 us -> 32.4 us (0.89)
  local copies, waits for them, and re-layouts: 2.85 us -> 0 us
  blocking collectives: 26.5 us -> 25.2 us
  Pallas kernels: 5.23 us -> 6.23 us
  other arithmetic: 0.68 us -> 0 us
    unnamed x8 -> x0, local copies, waits for them, and re-layouts: 2.34 us -> none
    all_to_all x1, blocking collectives: 17.2 us -> 16.2 us  [per_device(): lax.all_to_all(send.reshape(devices, height, lanes), ('src', 'tile'), 0, 0)]
    pallas_call x1, Pallas kernels: 0.22 us -> 1.05 us  [per_device(): pl.pallas_call(functools.partial(send_kernel, rim), out_shape=jax.ShapeDt...]
    all_to_all x1 -> x0, other arithmetic: 0.68 us -> none  [per_device(): lax.all_to_all(image.reshape(devices, rows, mine), ('src', 'tile'), 0, 0)]
    all_to_all x1 -> x0, local copies, waits for them, and re-layouts: 0.51 us -> none  [per_device(): lax.all_to_all(image.reshape(devices, rows, mine), ('src', 'tile'), 0, 0)]
where the time goes in v3:
time: 32.4 us; the launch traced here: 32.1 us
  blocking collectives  25.2 us (78%)
  Pallas kernels  6.23 us (19%)
  between operations  0.67 us (2%)
    all_to_all x1, blocking collectives, per_device(): lax.all_to_all(send.reshape(devices, height, lanes), ('src', 'tile'), 0, 0)  16.2 us
    all_to_all x1, blocking collectives, per_device(): lax.all_to_all(image.reshape((devices,) + image.shape[2:]), ('src', 'tile...  9.07 us
    pallas_call x1, Pallas kernels, per_device(): pl.pallas_call(functools.partial(image_kernel, rim, comps, rows, ranks),...  4.41 us
    pallas_call x1, Pallas kernels, per_device(): pl.pallas_call(functools.partial(send_kernel, rim), out_shape=jax.ShapeDt...  1.05 us
    pallas_call x1, Pallas kernels, per_device(): pl.pallas_call(merge_kernel, out_shape=jax.ShapeDtypeStruct((1, rows, wid...  0.78 us

profile of v3, /device:TPU:0, one launch (start us, length us, event | category | flops | bytes accessed | tf_op | source)
XLA Modules:
  0.0 32.1 jit_solution(6803856964189315872)
XLA Ops:
  0.7 1.0 %send_columns.1 = bf16[8,2,24,256]{3,2,1,0:T(8,128)(2,1)S(1)} custom-call(bf16[1,8,3,2,512]{4,3,2,1,0:T(2,128)(2,1)} %bitcast.7, bf16[1,2,8,65]{3,2,1,0:T(8,128)(2,1)} %x_taps_hbm.1, bf16[1,2,8,65]{3,2,1,0:T(8,128)(2,1)} %y_taps_hbm.1, f32[1]{0:T(128)S(6)} %copy.5.weight_ref), custom_call_target="tpu_custom_call" | custom-call | tf_op jit(solution)/shard_map/send_columns/pallas_call | solution.py:181
  1.7 16.2 %all_to_all.10 = bf16[16,24,256]{2,1,0:T(8,128)(2,1)S(1)} all-to-all(bf16[16,24,256]{2,1,0:T(8,128)(2,1)S(1)} %bitcast.5), channel_id=1, replica_groups=mesh['group'=2,'src'=8,'tile'=2] {'src','tile'}, dimensions={0} | all-to-all | bytes 393216 | tf_op jit(solution)/shard_map/all_to_all | solution.py:195
  17.9 4.4 %image.1 = f32[8,2,2,128]{3,2,1,0:T(2,128)S(1)} custom-call(bf16[8,2,24,256]{3,2,1,0:T(8,128)(2,1)S(1)} %bitcast.4), custom_call_target="tpu_custom_call" | custom-call | tf_op jit(solution)/shard_map/image/pallas_call | solution.py:197
  22.3 9.1 %all_to_all.11.parts_ref = f32[16,2,128]{2,1,0:T(2,128)S(1)} all-to-all(f32[16,2,128]{2,1,0:T(2,128)S(1)} %bitcast.6), channel_id=1, replica_groups=mesh['group'=2,'src'=8,'tile'=2] {'src','tile'}, dimensions={0} | all-to-all | bytes 32768 | tf_op jit(solution)/shard_map/all_to_all | solution.py:211
  31.4 0.8 %merge_columns.1 = f32[1,8,512]{2,1,0:T(8,128)} custom-call(f32[16,2,128]{2,1,0:T(2,128)S(1)} %all_to_all.11.parts_ref), custom_call_target="tpu_custom_call" | custom-call | tf_op jit(solution)/shard_map/merge_columns/pallas_call | solution.py:212

commit v4 on v3

--- a/solution.py
+++ b/solution.py
@@ -104,21 +104,20 @@
         ).astype(BF16)
         passed = lax.dot_general(column_mat, field_ref[...], (((1,), (1,)), ((), ())), preferred_element_type=F32)
         for chunk in range(chunks):
-            for n in range(2 * ranks):
-                cells = [
-                    passed[n * mine : (n + 1) * mine, comp * slab_rows + chunk * LANES : comp * slab_rows + (chunk + 1) * LANES]
-                    for comp in range(comps)
-                ]
-                lhs_ref[slot, chunk, :, n * LANES : (n + 1) * LANES] = jnp.concatenate(cells, axis=0).astype(BF16)
+            for r in range(ranks):
+                cells = []
+                for part in range(2):
+                    for comp in range(comps):
+                        top, left = (2 * r + part) * mine, comp * slab_rows + chunk * LANES
+                        cells.append(passed[top : top + mine, left : left + LANES])
+                lhs_ref[slot, chunk, :, r * LANES : (r + 1) * LANES] = jnp.concatenate(cells, axis=0).astype(BF16)
         for r in range(ranks):
-            re, im = (rolled(lines[r : r + 1], LANES) for lines in y_lines)
-            at = 2 * r * LANES
-            for n, mask in enumerate(masks):
-                re_n, im_n = jnp.where(mask, re, 0.0), jnp.where(mask, im, 0.0)
-                row_ref[slot, n, at : at + LANES, :LANES] = re_n.astype(BF16)
-                row_ref[slot, n, at : at + LANES, LANES:] = im_n.astype(BF16)
-                row_ref[slot, n, at + LANES : at + 2 * LANES, :LANES] = (-im_n).astype(BF16)
-                row_ref[slot, n, at + LANES : at + 2 * LANES, LANES:] = re_n.astype(BF16)
+            for part in range(2):
+                ring = rolled(y_lines[part][r : r + 1], LANES)
+                for n, mask in enumerate(masks):
+                    row_ref[slot, n, r * LANES : (r + 1) * LANES, part * LANES : (part + 1) * LANES] = jnp.where(
+                        mask, ring, 0.0
+                    ).astype(BF16)
         for chunk in range(chunks):
             image = None
             for n in range(windows):
@@ -126,8 +125,10 @@
                 if 0 <= other < chunks:
                     term = jnp.dot(lhs_ref[slot, other], row_ref[slot, n], preferred_element_type=F32)
                     image = term if image is None else image + term
-            square = image * image
-            square = square[:, :LANES] + square[:, LANES:]
+            of_re, of_im = image[: comps * mine], image[comps * mine :]
+            image_re = of_re[:, :LANES] - of_im[:, LANES:]
+            image_im = of_re[:, LANES:] + of_im[:, :LANES]
+            square = image_re * image_re + image_im * image_im
             power = square[:mine]
             for comp in range(1, comps):
                 power = power + square[comp * mine : (comp + 1) * mine]
@@ -201,8 +202,8 @@
         out_specs=whole,
         scratch_shapes=[
             pltpu.VMEM((comps * slab_rows, lanes), BF16),
-            pltpu.VMEM((slots, chunks, comps * mine, 2 * ranks * LANES), BF16),
-            pltpu.VMEM((slots, windows, 2 * ranks * LANES, 2 * LANES), BF16),
+            pltpu.VMEM((slots, chunks, 2 * comps * mine, ranks * LANES), BF16),
+            pltpu.VMEM((slots, windows, ranks * LANES, 2 * LANES), BF16),
             pltpu.VMEM((mine, slab_rows), F32),
         ],
         compiler_params=params,

time: 32.4 us -> 32 us (0.988)
  Pallas kernels: 6.23 us -> 5.87 us
    pallas_call x1, Pallas kernels: 4.41 us -> 4.04 us  [per_device(): pl.pallas_call(functools.partial(image_kernel, rim, comps, rows, ranks),...]
where the time goes in v4:
time: 32 us; the launch traced here: 31.8 us
  blocking collectives  25.2 us (79%)
  Pallas kernels  5.87 us (18%)
  between operations  0.67 us (2%)
    all_to_all x1, blocking collectives, per_device(): lax.all_to_all(send.reshape(devices, height, lanes), ('src', 'tile'), 0, 0)  16.2 us
    all_to_all x1, blocking collectives, per_device(): lax.all_to_all(image.reshape((devices,) + image.shape[2:]), ('src', 'tile...  9.07 us
    pallas_call x1, Pallas kernels, per_device(): pl.pallas_call(functools.partial(image_kernel, rim, comps, rows, ranks),...  4.04 us
    pallas_call x1, Pallas kernels, per_device(): pl.pallas_call(functools.partial(send_kernel, rim), out_shape=jax.ShapeDt...  1.05 us
    pallas_call x1, Pallas kernels, per_device(): pl.pallas_call(merge_kernel, out_shape=jax.ShapeDtypeStruct((1, rows, wid...  0.78 us

profile of v4, /device:TPU:0, one launch (start us, length us, event | category | flops | bytes accessed | tf_op | source)
XLA Modules:
  0.0 31.8 jit_solution(17387657490434272701)
XLA Ops:
  0.7 1.0 %send_columns.1 = bf16[8,2,24,256]{3,2,1,0:T(8,128)(2,1)S(1)} custom-call(bf16[1,8,3,2,512]{4,3,2,1,0:T(2,128)(2,1)} %bitcast.7, bf16[1,2,8,65]{3,2,1,0:T(8,128)(2,1)} %x_taps_hbm.1, bf16[1,2,8,65]{3,2,1,0:T(8,128)(2,1)} %y_taps_hbm.1, f32[1]{0:T(128)S(6)} %copy.5.weight_ref), custom_call_target="tpu_custom_call" | custom-call | tf_op jit(solution)/shard_map/send_columns/pallas_call | solution.py:182
  1.7 16.2 %all_to_all.10 = bf16[16,24,256]{2,1,0:T(8,128)(2,1)S(1)} all-to-all(bf16[16,24,256]{2,1,0:T(8,128)(2,1)S(1)} %bitcast.5), channel_id=1, replica_groups=mesh['group'=2,'src'=8,'tile'=2] {'src','tile'}, dimensions={0} | all-to-all | bytes 393216 | tf_op jit(solution)/shard_map/all_to_all | solution.py:196
  17.9 4.0 %image.1 = f32[8,2,2,128]{3,2,1,0:T(2,128)S(1)} custom-call(bf16[8,2,24,256]{3,2,1,0:T(8,128)(2,1)S(1)} %bitcast.4), custom_call_target="tpu_custom_call" | custom-call | tf_op jit(solution)/shard_map/image/pallas_call | solution.py:198
  21.9 9.1 %all_to_all.11.parts_ref = f32[16,2,128]{2,1,0:T(2,128)S(1)} all-to-all(f32[16,2,128]{2,1,0:T(2,128)S(1)} %bitcast.6), channel_id=1, replica_groups=mesh['group'=2,'src'=8,'tile'=2] {'src','tile'}, dimensions={0} | all-to-all | bytes 32768 | tf_op jit(solution)/shard_map/all_to_all | solution.py:212
  31.0 0.8 %merge_columns.1 = f32[1,8,512]{2,1,0:T(8,128)} custom-call(f32[16,2,128]{2,1,0:T(2,128)S(1)} %all_to_all.11.parts_ref), custom_call_target="tpu_custom_call" | custom-call | tf_op jit(solution)/shard_map/merge_columns/pallas_call | solution.py:213
